TPU v7x, 512 devices: a whole 4x4x16 slice. The times are simulated.
512 devices in a mesh: grp: 4 (over y_hi, core), seq: 16 (over z), kv: 8 (over x, y_lo).
Axes of the slice: x: 4, y: 4 (y_hi: 2, y_lo: 2; y = y_hi * 2 + y_lo), z: 16, core: 2. Of those that a mesh axis runs over, the one named last changes fastest.
Arguments:
- queries: bfloat16 [16384, 8192], P(('grp', 'seq'), 'kv'), parts along dimension 0, may hold values from -4.5 to 4.5
- resp_keys: bfloat16 [16384, 1024], P(('grp', 'seq'), 'kv'), parts along dimension 0, may hold values from -4.5 to 4.5
- resp_values: bfloat16 [16384, 1024], P(('grp', 'seq'), 'kv'), parts along dimension 0, may hold values from -4.5 to 4.5
- prompt_keys: bfloat16 [8192, 1024], P(('grp', 'seq'), 'kv'), parts along dimension 0, may hold values from -4.5 to 4.5
- prompt_values: bfloat16 [8192, 1024], P(('grp', 'seq'), 'kv'), parts along dimension 0, may hold values from -4.5 to 4.5
- outputs: bfloat16 [16384, 8192], P(('grp', 'seq'), 'kv'), parts along dimension 0, may hold values from -5 to 5
- out_grads: bfloat16 [16384, 8192], P(('grp', 'seq'), 'kv'), parts along dimension 0, may hold values from -24 to 24
- lengths: int32 [64], P(('grp', 'seq')), parts along dimension 0, may hold values from 1 to 256, 2048 in all
Outputs:
- query_grads: bfloat16 [16384, 8192], P(('grp', 'seq'), 'kv'), parts along dimension 0
- resp_key_grads: bfloat16 [16384, 1024], P(('grp', 'seq'), 'kv'), parts along dimension 0
- resp_value_grads: bfloat16 [16384, 1024], P(('grp', 'seq'), 'kv'), parts along dimension 0
- prompt_key_grads: bfloat16 [8192, 1024], P(('grp', 'seq'), 'kv'), parts along dimension 0
- prompt_value_grads: bfloat16 [8192, 1024], P(('grp', 'seq'), 'kv'), parts along dimension 0
There are 4 independent parts, one for each index of `grp`. A program takes and returns all parts, laid end to end along the dimension named above; each array names one. Nothing has to cross between parts.
Inputs may be any that keep to these rules, and one draw needn't show every extreme that they name: `lengths`: some response of each group has exactly 256 live tokens.
All inputs are finite; a program needn't handle non-finite values.
Results may differ from a plain program's by a relative error of at most 0.025.
Values may be sent and summed in bfloat16 or wider, within the bound.
A program may use at most 64 MiB of HBM per device.

v0:
```python
import jax
import jax.numpy as jnp
from jax import lax
from jax.sharding import PartitionSpec as P


def per_device(
    queries, resp_keys, resp_values, prompt_keys, prompt_values, outputs, out_grads, lengths
):
    rows = queries.shape[0]
    head_dim = resp_keys.shape[1]
    heads = queries.shape[1] // head_dim
    scale = head_dim ** (-0.5)
    group = min(heads, max(1, 512 // rows))
    while heads % group:
        group = group - 1
    blocks = heads // group
    prompt_keys_all, prompt_values_all = (
        lax.all_gather(prompt_keys, "seq", axis=0, tiled=True),
        lax.all_gather(prompt_values, "seq", axis=0, tiled=True),
    )
    prompt_rows = prompt_keys_all.shape[0]
    keys = jnp.concatenate([prompt_keys_all, resp_keys], 0)
    values = jnp.concatenate([prompt_values_all, resp_values], 0)
    row_pos = jnp.arange(rows, dtype=jnp.int32)
    live = row_pos < lengths[0]
    masked = jnp.where(live[:, None], out_grads, jnp.zeros_like(out_grads))
    query3 = queries.reshape(rows, heads, head_dim)
    grad3 = masked.reshape(rows, heads, head_dim)
    out3 = outputs.reshape(rows, heads, head_dim)
    key_pos = jnp.arange(keys.shape[0], dtype=jnp.int32) - prompt_rows
    allowed = key_pos[None, :] <= row_pos[:, None]
    kept_rows = keys.shape[0]

    def main_step(carry, index):
        query_blk = lax.dynamic_slice_in_dim(query3, index * group, group, 1)
        grad_blk = lax.dynamic_slice_in_dim(grad3, index * group, group, 1)
        out_blk = lax.dynamic_slice_in_dim(out3, index * group, group, 1)
        scores = (
            jnp.einsum("rhd,kd->hrk", query_blk, keys, preferred_element_type=jnp.float32) * scale
        )
        scores = jnp.where(allowed[None], scores, -jnp.inf)
        peak = jnp.max(scores, axis=2, keepdims=True)
        lse = peak + jnp.log(jnp.sum(jnp.exp(scores - peak), axis=2, keepdims=True))
        probs = jnp.exp(scores - lse)
        dprob = jnp.einsum("rhd,kd->hrk", grad_blk, values, preferred_element_type=jnp.float32)
        delta = jnp.einsum("rhd,rhd->hr", grad_blk, out_blk, preferred_element_type=jnp.float32)
        dscore = (probs * (dprob - delta[:, :, None]) * scale).astype(jnp.bfloat16)
        dquery = jnp.einsum("hrk,kd->rhd", dscore, keys, preferred_element_type=jnp.float32).astype(
            jnp.bfloat16
        )
        kept_probs = probs.astype(jnp.bfloat16)
        dkeys = carry[0] + jnp.einsum(
            "hrk,rhd->kd", dscore, query_blk, preferred_element_type=jnp.float32
        )
        dvalues = carry[1] + jnp.einsum(
            "hrk,rhd->kd", kept_probs, grad_blk, preferred_element_type=jnp.float32
        )
        return ((dkeys, dvalues), (dquery, lse[:, :, 0], delta))

    start = (
        jnp.zeros((kept_rows, head_dim), jnp.float32),
        jnp.zeros((kept_rows, head_dim), jnp.float32),
    )
    sums, stacked = lax.scan(main_step, start, jnp.arange(blocks))
    dquery_stack, lse_stack, delta_stack = stacked
    query_grads = jnp.moveaxis(dquery_stack, 0, 1).reshape(rows, heads * head_dim)
    resp_key_grads = sums[0][prompt_rows:].astype(jnp.bfloat16)
    resp_value_grads = sums[1][prompt_rows:].astype(jnp.bfloat16)
    summed_keys, summed_values = (
        lax.psum_scatter(
            sums[0][:prompt_rows].astype(jnp.bfloat16), "seq", scatter_dimension=0, tiled=True
        ).astype(jnp.float32),
        lax.psum_scatter(
            sums[1][:prompt_rows].astype(jnp.bfloat16), "seq", scatter_dimension=0, tiled=True
        ).astype(jnp.float32),
    )
    prompt_key_grads = summed_keys.astype(jnp.bfloat16)
    prompt_value_grads = summed_values.astype(jnp.bfloat16)
    return (query_grads, resp_key_grads, resp_value_grads, prompt_key_grads, prompt_value_grads)


def solution(mesh):
    return jax.shard_map(
        per_device,
        mesh=mesh,
        in_specs=(
            P(("grp", "seq"), "kv"),
            P(("grp", "seq"), "kv"),
            P(("grp", "seq"), "kv"),
            P(("grp", "seq"), "kv"),
            P(("grp", "seq"), "kv"),
            P(("grp", "seq"), "kv"),
            P(("grp", "seq"), "kv"),
            P(("grp", "seq")),
        ),
        out_specs=(
            P(("grp", "seq"), "kv"),
            P(("grp", "seq"), "kv"),
            P(("grp", "seq"), "kv"),
            P(("grp", "seq"), "kv"),
            P(("grp", "seq"), "kv"),
        ),
        check_vma=False,
    )
```

profile of v0, /device:TPU:6, one launch (start us, length us, event | category | flops | bytes accessed | tf_op | source)
XLA Modules:
  0.0 307.9 jit_solution(9428980621240812460)
XLA Ops:
  7.3 41.1 %all_gather.6 = bf16[2048,128]{1,0:T(8,128)(2,1)} all-gather(bf16[128,128]{1,0:T(8,128)(2,1)} %param.13), channel_id=1, replica_groups=mesh['grp'=4,'seq'=16,'kv'=8] {'seq'}, dimensions={0}, use_global_device_ids=true | all-gather | bytes 557056 | tf_op jit(solution)/shard_map/all_gather | solution.py:19
  48.4 31.4 %all_gather.7 = bf16[2048,128]{1,0:T(8,128)(2,1)} all-gather(bf16[128,128]{1,0:T(8,128)(2,1)} %param.14), channel_id=1, replica_groups=mesh['grp'=4,'seq'=16,'kv'=8] {'seq'}, dimensions={0}, use_global_device_ids=true | all-gather | bytes 557056 | tf_op jit(solution)/shard_map/all_gather | solution.py:20
  79.7 2.0 copy.19
  84.7 2.0 pad_maximum_fusion.1
  87.5 75.7 %while.15 = (s32[]{:T(128)}, f32[2304,128]{1,0:T(8,128)S(1)}, f32[2304,128]{1,0:T(8,128)S(1)}, bf16[4,256,2,128]{3,1,2,0:T(8,128)(2,1)}, s32[4]{0:T(128)S(1)}, /...) while((s32[]{:T(128)}, f32[2304,128]{1,0:T(8,128)S(1)}, ...), condition=%wide.region_3.4_spmd.clone, body=%wide.region_0.3_spmd.clone.sunk | while | flops 1526201344 | bytes 58689332 | solution.py:65
  91.2 1.3 copy-done
  93.4 3.7 %fusion.51 = f32[2304,128]{1,0:T(8,128)S(1)} fusion(bf16[256,2,128]{0,2,1:T(8,128)(2,1)S(1)} %constant_dynamic-slice_fusion.2, f32[2,256,2304]{2,1,0:T(8,128)} %copy-done, f32[2,256]{1,0:T(2,128)S(1)} %log_add_fusion.2, f32[2304,128]{1,0:T(8,128)S(1)} %get-tuple-element.229, pred[]{:T(512)S(6)} %compare.3), kind=kOutput, calls=%fused_computation.15.clone.1 | convolution fusion | flops 304939008 | bytes 7211009 | tf_op jit(solution)/shard_map/while/body/eval_jaxpr/hrk,rhd->kd/dot_general | solution.py:56
  97.3 1.4 multiply_reduce_fusion.2
  98.8 4.0 %fusion.49 = bf16[2,256,2304]{2,1,0:T(8,128)(2,1)S(1)} fusion(bf16[256,2,128]{0,2,1:T(8,128)(2,1)S(1)} %constant_dynamic-slice_fusion.2, f32[2,256,2304]{2,1,0:T(8,128)} %copy-done, f32[2,256]{1,0:T(2,128)S(1)} %copy.41, f32[2,256]{1,0:T(2,128)S(1)} %log_add_fusion.2, bf16[2304,128]{1,0:T(8,128)(2,1)} %get-tuple-element.250), kind=kOutput, calls=%fused_computation.10.clone.1 | convolution fusion | flops 307888128 | bytes 7802880 | tf_op jit(solution)/shard_map/while/body/eval_jaxpr/rhd,kd->hrk/dot_general | solution.py:46
  102.8 2.2 fusion.50
  105.0 1.4 fusion.52
  110.1 1.3 copy-done
  112.4 3.7 %fusion.51 = f32[2304,128]{1,0:T(8,128)S(1)} fusion(bf16[256,2,128]{0,2,1:T(8,128)(2,1)S(1)} %constant_dynamic-slice_fusion.2, f32[2,256,2304]{2,1,0:T(8,128)} %copy-done, f32[2,256]{1,0:T(2,128)S(1)} %log_add_fusion.2, f32[2304,128]{1,0:T(8,128)S(1)} %get-tuple-element.229, pred[]{:T(512)S(6)} %compare.3), kind=kOutput, calls=%fused_computation.15.clone.1 | convolution fusion | flops 304939008 | bytes 7211009 | tf_op jit(solution)/shard_map/while/body/eval_jaxpr/hrk,rhd->kd/dot_general | solution.py:56
  116.3 1.4 multiply_reduce_fusion.2
  117.8 4.0 %fusion.49 = bf16[2,256,2304]{2,1,0:T(8,128)(2,1)S(1)} fusion(bf16[256,2,128]{0,2,1:T(8,128)(2,1)S(1)} %constant_dynamic-slice_fusion.2, f32[2,256,2304]{2,1,0:T(8,128)} %copy-done, f32[2,256]{1,0:T(2,128)S(1)} %copy.41, f32[2,256]{1,0:T(2,128)S(1)} %log_add_fusion.2, bf16[2304,128]{1,0:T(8,128)(2,1)} %get-tuple-element.250), kind=kOutput, calls=%fused_computation.10.clone.1 | convolution fusion | flops 307888128 | bytes 7802880 | tf_op jit(solution)/shard_map/while/body/eval_jaxpr/rhd,kd->hrk/dot_general | solution.py:46
  121.7 2.2 fusion.50
  123.9 1.4 fusion.52
  129.0 1.3 copy-done
  131.3 3.7 %fusion.51 = f32[2304,128]{1,0:T(8,128)S(1)} fusion(bf16[256,2,128]{0,2,1:T(8,128)(2,1)S(1)} %constant_dynamic-slice_fusion.2, f32[2,256,2304]{2,1,0:T(8,128)} %copy-done, f32[2,256]{1,0:T(2,128)S(1)} %log_add_fusion.2, f32[2304,128]{1,0:T(8,128)S(1)} %get-tuple-element.229, pred[]{:T(512)S(6)} %compare.3), kind=kOutput, calls=%fused_computation.15.clone.1 | convolution fusion | flops 304939008 | bytes 7211009 | tf_op jit(solution)/shard_map/while/body/eval_jaxpr/hrk,rhd->kd/dot_general | solution.py:56
  135.2 1.4 multiply_reduce_fusion.2
  136.7 4.0 %fusion.49 = bf16[2,256,2304]{2,1,0:T(8,128)(2,1)S(1)} fusion(bf16[256,2,128]{0,2,1:T(8,128)(2,1)S(1)} %constant_dynamic-slice_fusion.2, f32[2,256,2304]{2,1,0:T(8,128)} %copy-done, f32[2,256]{1,0:T(2,128)S(1)} %copy.41, f32[2,256]{1,0:T(2,128)S(1)} %log_add_fusion.2, bf16[2304,128]{1,0:T(8,128)(2,1)} %get-tuple-element.250), kind=kOutput, calls=%fused_computation.10.clone.1 | convolution fusion | flops 307888128 | bytes 7802880 | tf_op jit(solution)/shard_map/while/body/eval_jaxpr/rhd,kd->hrk/dot_general | solution.py:46
  140.7 2.2 fusion.50
  142.9 1.4 fusion.52
  148.0 1.3 copy-done
  150.2 3.7 %fusion.51 = f32[2304,128]{1,0:T(8,128)S(1)} fusion(bf16[256,2,128]{0,2,1:T(8,128)(2,1)S(1)} %constant_dynamic-slice_fusion.2, f32[2,256,2304]{2,1,0:T(8,128)} %copy-done, f32[2,256]{1,0:T(2,128)S(1)} %log_add_fusion.2, f32[2304,128]{1,0:T(8,128)S(1)} %get-tuple-element.229, pred[]{:T(512)S(6)} %compare.3), kind=kOutput, calls=%fused_computation.15.clone.1 | convolution fusion | flops 304939008 | bytes 7211009 | tf_op jit(solution)/shard_map/while/body/eval_jaxpr/hrk,rhd->kd/dot_general | solution.py:56
  154.1 1.4 multiply_reduce_fusion.2
  155.6 4.0 %fusion.49 = bf16[2,256,2304]{2,1,0:T(8,128)(2,1)S(1)} fusion(bf16[256,2,128]{0,2,1:T(8,128)(2,1)S(1)} %constant_dynamic-slice_fusion.2, f32[2,256,2304]{2,1,0:T(8,128)} %copy-done, f32[2,256]{1,0:T(2,128)S(1)} %copy.41, f32[2,256]{1,0:T(2,128)S(1)} %log_add_fusion.2, bf16[2304,128]{1,0:T(8,128)(2,1)} %get-tuple-element.250), kind=kOutput, calls=%fused_computation.10.clone.1 | convolution fusion | flops 307888128 | bytes 7802880 | tf_op jit(solution)/shard_map/while/body/eval_jaxpr/rhd,kd->hrk/dot_general | solution.py:46
  159.6 2.2 fusion.50
  161.8 1.4 fusion.52
  166.4 1.6 copy.22
  169.1 61.4 %reduce-scatter.3.cloned.1.call-done = bf16[128,128]{1,0:T(8,128)(2,1)} async-done(((bf16[2048,128]{1,0:T(8,128)(2,1)}), bf16[128,128]{1,0:T(8,128)(2,1)}) %reduce-scatter.3.cloned.1.call-update) | async-done | bytes 32784 | tf_op jit(solution)/shard_map/reduce_scatter | solution.py:71
  230.5 70.6 %reduce-scatter.5.cloned.1.call-done = bf16[128,128]{1,0:T(8,128)(2,1)} async-done(((bf16[2048,128]{1,0:T(8,128)(2,1)}), bf16[128,128]{1,0:T(8,128)(2,1)}) %reduce-scatter.5.cloned.1.call-update) | async-done | bytes 32784 | tf_op jit(solution)/shard_map/reduce_scatter | solution.py:74
  (85 shorter events, 23.9 us)
Async XLA Ops:
  7.2 75.3 %copy-start.4 = (bf16[256,1024]{1,0:T(8,128)(2,1)S(1)}, bf16[256,1024]{1,0:T(8,128)(2,1)}, u32[]{:S(2)}) copy-start(bf16[256,1024]{1,0:T(8,128)(2,1)} %param.15) | copy-start | bytes 1572868
  7.2 76.2 %copy-start.5 = (bf16[256,1024]{1,0:T(8,128)(2,1)S(1)}, bf16[256,1024]{1,0:T(8,128)(2,1)}, u32[]{:S(2)}) copy-start(bf16[256,1024]{1,0:T(8,128)(2,1)} %param.10) | copy-start | bytes 1572868
  7.2 76.4 %copy-start.6 = (bf16[256,128]{1,0:T(8,128)(2,1)S(1)}, bf16[256,128]{1,0:T(8,128)(2,1)}, u32[]{:S(2)}) copy-start(bf16[256,128]{1,0:T(8,128)(2,1)} %param.11) | copy-start | bytes 196612
  7.2 223.3 %reduce-scatter.3.cloned.1.call-start = ((), (), s32[]{:S(2)}) async-start(), calls=%async_computation.2 | async-start | bytes 557056 | tf_op jit(solution)/shard_map/reduce_scatter | solution.py:71
  83.6 3.1 %copy-start.3 = (bf16[256,1024]{0,1:T(8,128)(2,1)S(1)}, bf16[256,1024]{0,1:T(8,128)(2,1)}, u32[]{:S(2)}) copy-start(bf16[256,1024]{0,1:T(8,128)(2,1)} %copy.19) | copy-start | bytes 1572868
  87.5 2.9 copy-start.1
  90.4 2.1 copy-start
  105.0 1.5 copy-start.2
  106.5 2.9 copy-start.1
  109.3 2.1 copy-start
  123.9 1.5 copy-start.2
  125.4 2.9 copy-start.1
  128.2 2.1 copy-start
  142.8 1.5 copy-start.2
  144.3 2.9 copy-start.1
  147.2 2.1 copy-start
  161.8 1.5 copy-start.2
  164.1 137.0 %reduce-scatter.5.cloned.1.call-start = ((), (), s32[]{:S(2)}) async-start(), calls=%async_computation.3 | async-start | bytes 557056 | tf_op jit(solution)/shard_map/reduce_scatter | solution.py:74
Sparse Core Ops, SparseCore 0:
  164.3 66.2 reduce-scatter.2
  234.1 66.9 reduce-scatter.4
where the time goes:
time: 309 us; the launch traced here: 308 us
  waiting for transfers between devices  132 us (43%)
  blocking collectives  72.5 us (23%)
  matrix products  50.2 us (16%)
  local copies, waits for them, and re-layouts  21.4 us (7%)
  between operations  14.8 us (5%)
  other arithmetic  14.1 us (5%)
    reduce_scatter x1, waiting for transfers between devices, per_device(): lax.psum_scatter(sums[1][:prompt_rows].astype(jnp.bfloat16), 'seq', scatt...  70.6 us
    reduce_scatter x1, waiting for transfers between devices, per_device(): lax.psum_scatter(sums[0][:prompt_rows].astype(jnp.bfloat16), 'seq', scatt...  61.4 us
    all_gather x1, blocking collectives, per_device(): lax.all_gather(prompt_keys, 'seq', axis=0, tiled=True)  41.1 us
    all_gather x1, blocking collectives, per_device(): lax.all_gather(prompt_values, 'seq', axis=0, tiled=True)  31.4 us
    dot_general x4, matrix products, main_step(): jnp.einsum('rhd,kd->hrk', grad_blk, values, preferred_element_type=jnp.fl...  15.9 us
    dot_general x4, matrix products, main_step(): jnp.einsum('hrk,rhd->kd', kept_probs, grad_blk, preferred_element_type=jn...  15 us
    dot_general x4, matrix products, main_step(): jnp.einsum('hrk,rhd->kd', dscore, query_blk, preferred_element_type=jnp.f...  8.74 us
  transfers between devices with their start and end apart: 2, of which 2 were waited for; matrix products, arithmetic and copies ran while one was open for 2% of the time, Pallas kernels for 0%

commit v1 on v0

v1 whole, which is shorter than its diff:
```python
import functools

import jax
import jax.numpy as jnp
from jax import lax
from jax.experimental import pallas as pl
from jax.experimental.pallas import tpu as pltpu
from jax.sharding import PartitionSpec as P

MESH = pl.DeviceIdType.MESH
F32 = jnp.float32
BF16 = jnp.bfloat16
LOG2E = 1.4426950408889634
LOW = -1e30
PARENT = {1: 0, 2: 0, 3: 2, 4: 2, 5: 4, 6: 4, 7: 6, 8: 6}
HU = 2


def dot(a, b):
    return jnp.dot(a, b, preferred_element_type=F32)


def split3(x):
    hi = x.astype(BF16).astype(F32)
    mid = (x - hi).astype(BF16).astype(F32)
    lo = ((x - hi) - mid).astype(BF16).astype(F32)
    row = lax.broadcasted_iota(jnp.int32, (16, x.shape[1]), 0)
    out = jnp.where(row == 0, hi, jnp.where(row == 1, mid, jnp.where(row == 2, lo, 0.0)))
    return out.astype(BF16)


def kernel(
    n, heads, scale,
    q_hbm, kr_hbm, vr_hbm, kp_hbm, vp_hbm, o_hbm, g_hbm, len_ref,
    dq_hbm, dkr_hbm, dvr_hbm, dkp_hbm, dvp_hbm,
    kv, q3, g3, o3, qt, gt, kt, ds, part, sums, got, dq3, resp_out, prompt_out, ext, m8, l8,
    ag_send, ag_recv, rs_send, rs_recv, in_sem, kv_sem, out_sem,
):
    c2 = scale * LOG2E
    rows = q3.shape[1]
    head_dim = q3.shape[2]
    chunk = 2 * head_dim
    me = lax.axis_index("seq")

    def at(step):
        return {"seq": lax.rem(me + step + n, n)}

    barrier = pltpu.get_barrier_semaphore()
    for step in (1, -1, 2, -2):
        pl.semaphore_signal(barrier, inc=1, device_id=at(step), device_id_type=MESH)

    own = 8 * chunk
    local = [
        pltpu.make_async_copy(kp_hbm, kv.at[0, pl.ds(own, 128)], kv_sem.at[0]),
        pltpu.make_async_copy(vp_hbm, kv.at[1, pl.ds(own, 128)], kv_sem.at[1]),
        pltpu.make_async_copy(kr_hbm, kv.at[0, pl.ds(0, chunk)], kv_sem.at[2]),
        pltpu.make_async_copy(vr_hbm, kv.at[1, pl.ds(0, chunk)], kv_sem.at[3]),
    ]
    for copy in local:
        copy.start()
    loads = []
    for h in range(heads):
        for a, (src, dst) in enumerate(((q_hbm, q3), (g_hbm, g3), (o_hbm, o3))):
            copy = pltpu.make_async_copy(
                src.at[:, pl.ds(h * head_dim, head_dim)], dst.at[h], in_sem.at[a, h]
            )
            copy.start()
            loads.append(copy)

    def slot(d, way):
        if d == 8:
            return pl.ds(own + 128 + 64 * way, 64)
        return pl.ds(d * chunk + 128 * way, 128)

    def gather(kind, d, way):
        pa = PARENT[d]
        step = (d - pa) * (1 if way == 0 else -1)
        if pa == 0:
            src = (kp_hbm, vp_hbm)[kind]
        elif d == 8:
            src = kv.at[kind, pl.ds(pa * chunk + 128 * way + 64 * way, 64)]
        else:
            src = kv.at[kind, slot(pa, way)]
        return pltpu.make_async_remote_copy(
            src_ref=src, dst_ref=kv.at[kind, slot(d, way)],
            send_sem=ag_send.at[kind, way, d - 1], recv_sem=ag_recv.at[kind, way, d - 1],
            device_id=at(step), device_id_type=MESH,
        )

    ag = {(k, d, w): gather(k, d, w) for k in range(2) for d in range(1, 9) for w in range(2)}

    pl.semaphore_wait(barrier, 4)
    for kind in range(2):
        for d in (2, 1):
            for way in range(2):
                ag[kind, d, way].start()

    lane = lax.broadcasted_iota(jnp.int32, (chunk, 128), 1)
    ext[...] = jnp.where(lane < 3, -1.0, 0.0).astype(BF16)
    qt[pl.ds(head_dim, 128), :] = jnp.zeros((128, qt.shape[1]), BF16)
    gt[pl.ds(head_dim, 128), :] = jnp.zeros((128, gt.shape[1]), BF16)
    m8[...] = jnp.full(m8.shape, LOW, F32)
    l8[...] = jnp.zeros(l8.shape, F32)
    for copy in loads:
        copy.wait()
    length = len_ref[0]
    live = lax.broadcasted_iota(jnp.int32, (rows, head_dim), 0) < length

    def cols(h):
        return pl.ds(pl.multiple_of(h * rows, rows), rows)

    def prepare(h, carry):
        q = q3[h].astype(F32)
        g = jnp.where(live, g3[h].astype(F32), 0.0)
        o = o3[h].astype(F32)
        g3[h] = g.astype(BF16)
        g_t = g.T
        delta = jnp.sum(g_t * o.T, axis=0, keepdims=True)
        qt[pl.ds(0, head_dim), cols(h)] = q.T.astype(BF16)
        gt[pl.ds(0, head_dim), cols(h)] = g_t.astype(BF16)
        gt[pl.ds(head_dim, 16), cols(h)] = split3(delta)
        return carry

    lax.fori_loop(0, heads, prepare, 0)

    def causal():
        key = lax.broadcasted_iota(jnp.int32, (chunk, rows), 0)
        token = lax.broadcasted_iota(jnp.int32, (chunk, rows), 1)
        return key <= token

    def chunk_rows(c):
        if isinstance(c, int):
            return pl.ds(c * chunk, chunk)
        return pl.ds(pl.multiple_of(c * chunk, chunk), chunk)

    def first_pass(c, masked=False):
        keys = kv[0, chunk_rows(c)]
        kt[:, chunk_rows(c)] = keys.astype(F32).T.astype(BF16)

        def step(h, carry):
            s = dot(keys, qt[pl.ds(0, head_dim), cols(h)])
            if masked:
                s = jnp.where(causal(), s, LOW)
            s = s.reshape(chunk // 8, 8, rows)
            old = m8[h]
            new = jnp.maximum(old, jnp.max(s, axis=0))
            e = jnp.exp2((s - new[None]) * c2)
            l8[h] = l8[h] * jnp.exp2((old - new) * c2) + jnp.sum(e, axis=0)
            m8[h] = new
            return carry

        lax.fori_loop(0, heads, step, 0, unroll=HU)

    def finish_first():
        def step(h, carry):
            m = jnp.max(m8[h], axis=0, keepdims=True)
            total = jnp.sum(l8[h] * jnp.exp2((m8[h] - m) * c2), axis=0, keepdims=True)
            lse = m + jnp.log(total) * (1.0 / scale)
            qt[pl.ds(head_dim, 16), cols(h)] = split3(lse)
            return carry

        lax.fori_loop(0, heads, step, 0, unroll=HU)

    def second_pass(c, masked=False):
        keys = jnp.concatenate([kv[0, chunk_rows(c)], ext[...]], axis=1)
        values = jnp.concatenate([kv[1, chunk_rows(c)], ext[...]], axis=1)
        zero = jnp.zeros((chunk, head_dim), F32)
        part[0, chunk_rows(c)] = zero
        part[1, chunk_rows(c)] = zero

        def step(h, carry):
            p = jnp.exp2(dot(keys, qt[:, cols(h)]) * c2)
            if masked:
                p = jnp.where(causal(), p, 0.0)
            dp = dot(values, gt[:, cols(h)])
            d_s = (p * dp).astype(BF16)
            ds[chunk_rows(c), cols(h)] = d_s
            part[1, chunk_rows(c)] += dot(p.astype(BF16), g3[h])
            part[0, chunk_rows(c)] += dot(d_s, q3[h])
            return carry

        lax.fori_loop(0, heads, step, 0, unroll=HU)

    local[2].wait()
    local[3].wait()
    first_pass(0, masked=True)
    local[0].wait()
    local[1].wait()

    def pair(hi, body):
        def step(i, carry):
            body(hi - i)
            return carry

        lax.fori_loop(0, 2, step, 0)

    for stage in (1, 2, 3, 4):
        if stage < 4:
            for kind in range(2):
                for way in range(2):
                    ag[kind, 2 * stage, way].wait_recv()
                    ag[kind, 2 * stage + 2, way].start()
                    ag[kind, 2 * stage + 1, way].start()
            for kind in range(2):
                for way in range(2):
                    ag[kind, 2 * stage - 1, way].wait_recv()
        else:
            for kind in range(2):
                for d in (8, 7):
                    for way in range(2):
                        ag[kind, d, way].wait_recv()
        pair(2 * stage, first_pass)
    finish_first()

    factor = (scale, 1.0)

    def mine(kind, d, way):
        if d == 0:
            r = pl.ds(own, 128)
        elif d == 8:
            r = pl.ds(own + 128 + 64 * way, 64)
        else:
            r = pl.ds(d * chunk + 128 * (1 - way), 128)
        return part[kind, r] * factor[kind]

    def rs_rows(d, way):
        return pl.ds(64 * way, 64) if d == 8 else pl.ds(0, 128)

    def scatter(kind, d, way):
        step = (d - PARENT[d]) * (1 if way == 0 else -1)
        r = rs_rows(d, way)
        return pltpu.make_async_remote_copy(
            src_ref=sums.at[kind, way, d - 1, r], dst_ref=got.at[kind, way, d - 1, r],
            send_sem=rs_send.at[kind, way, d - 1], recv_sem=rs_recv.at[kind, way, d - 1],
            device_id=at(step), device_id_type=MESH,
        )

    rs = {(k, d, w): scatter(k, d, w) for k in range(2) for d in range(1, 9) for w in range(2)}

    def total(kind, d, way, acc):
        for child in (8, 7, 6, 5, 4, 3, 2, 1):
            if PARENT[child] != d:
                continue
            rs[kind, child, way].wait_recv()
            term = got[kind, way, child - 1, rs_rows(child, way)].astype(F32)
            if child == 8:
                if way == 0:
                    acc = jnp.concatenate([acc[:64] + term, acc[64:]], axis=0)
                else:
                    acc = jnp.concatenate([acc[:64], acc[64:] + term], axis=0)
            else:
                acc = acc + term
        return acc

    def send_sum(kind, d, way):
        acc = total(kind, d, way, mine(kind, d, way))
        sums[kind, way, d - 1, rs_rows(d, way)] = acc.astype(BF16)
        rs[kind, d, way].start()

    for stage in (4, 3, 2, 1):
        pair(2 * stage, second_pass)
        for d in (2 * stage - 1, 2 * stage):
            for kind in (1, 0):
                for way in range(2):
                    send_sum(kind, d, way)

    second_pass(0, masked=True)
    resp_out[0] = (part[0, pl.ds(0, chunk)] * scale).astype(BF16)
    resp_out[1] = part[1, pl.ds(0, chunk)].astype(BF16)
    outs = [
        pltpu.make_async_copy(resp_out.at[0], dkr_hbm, kv_sem.at[0]),
        pltpu.make_async_copy(resp_out.at[1], dvr_hbm, kv_sem.at[1]),
    ]
    for copy in outs:
        copy.start()

    def query_grad(h, carry):
        d_q = dot(kt[...], ds[:, cols(h)]) * scale
        dq3[h] = d_q.T.astype(BF16)
        return carry

    lax.fori_loop(0, heads, query_grad, 0, unroll=HU)
    for h in range(heads):
        copy = pltpu.make_async_copy(
            dq3.at[h], dq_hbm.at[:, pl.ds(h * head_dim, head_dim)], out_sem.at[h]
        )
        copy.start()
        outs.append(copy)

    for kind in (1, 0):
        acc = mine(kind, 0, 0)
        for way in range(2):
            acc = total(kind, 0, way, acc)
        prompt_out[kind] = acc.astype(BF16)
        copy = pltpu.make_async_copy(
            prompt_out.at[kind], (dkp_hbm, dvp_hbm)[kind], kv_sem.at[2 + kind]
        )
        copy.start()
        outs.append(copy)

    for copy in ag.values():
        copy.wait_send()
    for copy in rs.values():
        copy.wait_send()
    for copy in outs:
        copy.wait()


def per_device(n, queries, resp_keys, resp_values, prompt_keys, prompt_values, outputs, out_grads, lengths):
    rows = queries.shape[0]
    head_dim = resp_keys.shape[1]
    heads = queries.shape[1] // head_dim
    scale = head_dim ** (-0.5)
    keys = n * prompt_keys.shape[0] + rows
    wide = heads * rows
    any_spec = pl.BlockSpec(memory_space=pl.ANY)
    shape = jax.ShapeDtypeStruct
    return pl.pallas_call(
        functools.partial(kernel, n, heads, scale),
        out_shape=(
            shape(queries.shape, BF16),
            shape(resp_keys.shape, BF16),
            shape(resp_values.shape, BF16),
            shape(prompt_keys.shape, BF16),
            shape(prompt_values.shape, BF16),
        ),
        in_specs=[any_spec] * 7 + [pl.BlockSpec(memory_space=pltpu.SMEM)],
        out_specs=(any_spec,) * 5,
        scratch_shapes=[
            pltpu.VMEM((2, keys, head_dim), BF16),
            pltpu.VMEM((heads, rows, head_dim), BF16),
            pltpu.VMEM((heads, rows, head_dim), BF16),
            pltpu.VMEM((heads, rows, head_dim), BF16),
            pltpu.VMEM((2 * head_dim, wide), BF16),
            pltpu.VMEM((2 * head_dim, wide), BF16),
            pltpu.VMEM((head_dim, keys), BF16),
            pltpu.VMEM((keys, wide), BF16),
            pltpu.VMEM((2, keys, head_dim), F32),
            pltpu.VMEM((2, 2, 8, 128, head_dim), BF16),
            pltpu.VMEM((2, 2, 8, 128, head_dim), BF16),
            pltpu.VMEM((heads, rows, head_dim), BF16),
            pltpu.VMEM((2, rows, head_dim), BF16),
            pltpu.VMEM((2, 128, head_dim), BF16),
            pltpu.VMEM((2 * head_dim, 128), BF16),
            pltpu.VMEM((heads, 8, rows), F32),
            pltpu.VMEM((heads, 8, rows), F32),
            pltpu.SemaphoreType.DMA((2, 2, 8)),
            pltpu.SemaphoreType.DMA((2, 2, 8)),
            pltpu.SemaphoreType.DMA((2, 2, 8)),
            pltpu.SemaphoreType.DMA((2, 2, 8)),
            pltpu.SemaphoreType.DMA((3, heads)),
            pltpu.SemaphoreType.DMA((4,)),
            pltpu.SemaphoreType.DMA((heads,)),
        ],
        compiler_params=pltpu.CompilerParams(
            collective_id=0, has_side_effects=True, vmem_limit_bytes=48 * 1024 * 1024
        ),
    )(queries, resp_keys, resp_values, prompt_keys, prompt_values, outputs, out_grads, lengths)


def solution(mesh):
    spec = P(("grp", "seq"), "kv")
    return jax.shard_map(
        functools.partial(per_device, mesh.shape["seq"]),
        mesh=mesh,
        in_specs=(spec,) * 7 + (P(("grp", "seq")),),
        out_specs=(spec,) * 5,
        check_vma=False,
    )
```

time: 309 us -> 74.2 us (0.24)
  waiting for transfers between devices: 132 us -> 0 us
  blocking collectives: 72.5 us -> 0 us
  Pallas kernels: 0 us -> 61.8 us
  matrix products: 50.2 us -> 0 us
  other arithmetic: 14.1 us -> 0 us
  between operations: 14.8 us -> 1.31 us
  local copies, waits for them, and re-layouts: 21.4 us -> 9.59 us
    reduce_scatter x2 -> x0, waiting for transfers between devices: 132 us -> none  [the longest x1 70.6 us: per_device(): lax.psum_scatter(sums[1][:prompt_rows].astype(jnp.bfloat16), 'seq', scatt...]
    all_gather x2 -> x0, blocking collectives: 72.5 us -> none  [the longest x1 41.1 us: per_device(): lax.all_gather(prompt_keys, 'seq', axis=0, tiled=True)]
    pallas_call x0 -> x1, Pallas kernels: none -> 61.8 us  [per_device(): pl.pallas_call(functools.partial(kernel, n, heads, scale), out_shape=(sha...]
    dot_general x20 -> x0, matrix products: 50.2 us -> none  [the longest x4 15.9 us: main_step(): jnp.einsum('rhd,kd->hrk', grad_blk, values, preferred_element_type=jnp.fl...]
    dynamic_slice x12 -> x0, local copies, waits for them, and re-layouts: 6.85 us -> none  [the longest x8 4.15 us: main_step(): grad_blk = lax.dynamic_slice_in_dim(grad3, index * group, group, 1)]
    unnamed x11 -> x19, local copies, waits for them, and re-layouts: 3.16 us -> 9.59 us
    while x8 -> x0, other arithmetic: 5.69 us -> none
    while x24 -> x0, local copies, waits for them, and re-layouts: 5.38 us -> none
  transfers between devices with their start and end apart: 2 -> 0, of which waited for: 2 -> 0; matrix products, arithmetic and copies ran while one was open for 2% -> 0% of each run, Pallas kernels for 0% -> 0%
where the time goes in v1:
time: 74.2 us; the launch traced here: 72.7 us
  Pallas kernels  61.8 us (83%)
  local copies, waits for them, and re-layouts  9.59 us (13%)
  between operations  1.31 us (2%)
    pallas_call x1, Pallas kernels, per_device(): pl.pallas_call(functools.partial(kernel, n, heads, scale), out_shape=(sha...  61.8 us
    unnamed x19, local copies, waits for them, and re-layouts  9.59 us

profile of v1, /device:TPU:6, one launch (start us, length us, event | category | flops | bytes accessed | tf_op | source)
XLA Modules:
  0.0 72.7 jit_solution(6656110879463176912)
XLA Ops:
  1.3 0.0 copy-start
  1.3 1.0 %copy-done = bf16[256,1024]{1,0:T(8,128)(2,1)S(1)} copy-done((bf16[256,1024]{1,0:T(8,128)(2,1)S(1)}, bf16[256,1024]{1,0:T(8,128)(2,1)}, u32[]{:S(2)}) %copy-start) | copy-done | bytes 524312
  2.3 0.0 copy-start.1
  2.3 1.0 %copy-done.1 = bf16[256,1024]{1,0:T(8,128)(2,1)S(1)} copy-done((bf16[256,1024]{1,0:T(8,128)(2,1)S(1)}, bf16[256,1024]{1,0:T(8,128)(2,1)}, u32[]{:S(2)}) %copy-start.1) | copy-done | bytes 524312
  3.4 0.0 copy-start.2
  3.4 1.0 %copy-done.2 = bf16[256,1024]{1,0:T(8,128)(2,1)S(1)} copy-done((bf16[256,1024]{1,0:T(8,128)(2,1)S(1)}, bf16[256,1024]{1,0:T(8,128)(2,1)}, u32[]{:S(2)}) %copy-start.2) | copy-done | bytes 524312
  4.4 0.0 copy-start.3
  4.4 0.8 %copy-done.3 = bf16[256,128]{1,0:T(8,128)(2,1)S(1)} copy-done((bf16[256,128]{1,0:T(8,128)(2,1)S(1)}, bf16[256,128]{1,0:T(8,128)(2,1)}, u32[]{:S(2)}) %copy-start.3) | copy-done | bytes 65560
  5.2 0.0 copy-start.4
  5.2 0.8 %copy-done.4 = bf16[256,128]{1,0:T(8,128)(2,1)S(1)} copy-done((bf16[256,128]{1,0:T(8,128)(2,1)S(1)}, bf16[256,128]{1,0:T(8,128)(2,1)}, u32[]{:S(2)}) %copy-start.4) | copy-done | bytes 65560
  6.1 0.0 copy-start.5
  6.1 0.8 %copy-done.5 = bf16[128,128]{1,0:T(8,128)(2,1)S(1)} copy-done((bf16[128,128]{1,0:T(8,128)(2,1)S(1)}, bf16[128,128]{1,0:T(8,128)(2,1)}, u32[]{:S(2)}) %copy-start.5) | copy-done | bytes 32792
  6.8 0.0 copy-start.6
  6.8 0.8 %copy-done.6 = bf16[128,128]{1,0:T(8,128)(2,1)S(1)} copy-done((bf16[128,128]{1,0:T(8,128)(2,1)S(1)}, bf16[128,128]{1,0:T(8,128)(2,1)}, u32[]{:S(2)}) %copy-start.6) | copy-done | bytes 32792
  7.6 61.8 %shard_map.119 = (bf16[256,1024]{1,0:T(8,128)(2,1)S(1)}, bf16[256,128]{1,0:T(8,128)(2,1)S(1)}, bf16[256,128]{1,0:T(8,128)(2,1)S(1)}, bf16[128,128]{1,0:T(8,128)(2,1)S(1)}, bf16[128,128]{1,0:T(8,128)(2,1)S(1)}) custom-call(bf16[256,1024]{1,0:T(8,128)(2,1)S(1)} %copy-done, bf16[256,128]{1,0:T(8,128)(2,1)S(1)} %copy-done.3, bf16[256,128]{1,0:T(8,128)(2,1)S(1)} %copy-done.4, ...), custom_call_target="tpu_custom_call" | custom-call | tf_op jit(solution)/shard_map/pallas_call | solution.py:318
  69.4 0.8 %copy.19 = bf16[256,1024]{1,0:T(8,128)(2,1)} copy(bf16[256,1024]{1,0:T(8,128)(2,1)S(1)} %get-tuple-element.10) | data formatting | bytes 1048576
  70.2 0.6 copy.20
  70.9 0.6 copy.21
  71.5 0.6 copy.22
  72.1 0.6 copy.23
Async XLA Ops:
  1.3 1.0 %copy-start = (bf16[256,1024]{1,0:T(8,128)(2,1)S(1)}, bf16[256,1024]{1,0:T(8,128)(2,1)}, u32[]{:S(2)}) copy-start(bf16[256,1024]{1,0:T(8,128)(2,1)} %q_hbm.1) | copy-start | bytes 1572868
  2.3 1.0 %copy-start.1 = (bf16[256,1024]{1,0:T(8,128)(2,1)S(1)}, bf16[256,1024]{1,0:T(8,128)(2,1)}, u32[]{:S(2)}) copy-start(bf16[256,1024]{1,0:T(8,128)(2,1)} %o_hbm.1) | copy-start | bytes 1572868
  3.4 1.0 %copy-start.2 = (bf16[256,1024]{1,0:T(8,128)(2,1)S(1)}, bf16[256,1024]{1,0:T(8,128)(2,1)}, u32[]{:S(2)}) copy-start(bf16[256,1024]{1,0:T(8,128)(2,1)} %g_hbm.1) | copy-start | bytes 1572868
  4.4 0.8 %copy-start.3 = (bf16[256,128]{1,0:T(8,128)(2,1)S(1)}, bf16[256,128]{1,0:T(8,128)(2,1)}, u32[]{:S(2)}) copy-start(bf16[256,128]{1,0:T(8,128)(2,1)} %kr_hbm.1) | copy-start | bytes 196612
  5.2 0.8 %copy-start.4 = (bf16[256,128]{1,0:T(8,128)(2,1)S(1)}, bf16[256,128]{1,0:T(8,128)(2,1)}, u32[]{:S(2)}) copy-start(bf16[256,128]{1,0:T(8,128)(2,1)} %vr_hbm.1) | copy-start | bytes 196612
  6.1 0.8 %copy-start.5 = (bf16[128,128]{1,0:T(8,128)(2,1)S(1)}, bf16[128,128]{1,0:T(8,128)(2,1)}, u32[]{:S(2)}) copy-start(bf16[128,128]{1,0:T(8,128)(2,1)} %kp_hbm.1) | copy-start | bytes 98308
  6.8 0.8 %copy-start.6 = (bf16[128,128]{1,0:T(8,128)(2,1)S(1)}, bf16[128,128]{1,0:T(8,128)(2,1)}, u32[]{:S(2)}) copy-start(bf16[128,128]{1,0:T(8,128)(2,1)} %vp_hbm.1) | copy-start | bytes 98308

commit v2 on v1

v2 whole, which is shorter than its diff:
```python
import functools

import jax
import jax.numpy as jnp
from jax import lax
from jax.experimental import pallas as pl
from jax.experimental.pallas import tpu as pltpu
from jax.sharding import PartitionSpec as P

MESH = pl.DeviceIdType.MESH
F32 = jnp.float32
BF16 = jnp.bfloat16
LOG2E = 1.4426950408889634
LOW = -1e30
PARENT = {1: 0, 2: 0, 3: 2, 4: 2, 5: 4, 6: 4, 7: 6, 8: 6}
ROUNDS = (
    (">k2,k1,v2",),
    ("k2>k4,k3", "v2>v4,v1", "k1"),
    ("k4>k6,k5", "v4>v6,v3", "k3"),
    ("k6>k8,k7", "v6>v8,v7,v5", "k5"),
    ("k8", "k7"),
)
PLAN = (
    ("v8", "v7"),
    ("k8", "k7"),
    ("v5", "v6"),
    ("k5", "k6"),
    ("v3", "v4"),
    ("k3", "k4"),
    ("v1", "v2"),
    ("k1", "k2"),
    (),
    (),
)
HU = 8


def dot(a, b):
    return jnp.dot(a, b, preferred_element_type=F32)


def split3(x):
    hi = x.astype(BF16).astype(F32)
    mid = (x - hi).astype(BF16).astype(F32)
    lo = ((x - hi) - mid).astype(BF16).astype(F32)
    row = lax.broadcasted_iota(jnp.int32, (16, x.shape[1]), 0)
    out = jnp.where(row == 0, hi, jnp.where(row == 1, mid, jnp.where(row == 2, lo, 0.0)))
    return out.astype(BF16)


def kernel(
    n, heads, scale,
    q_hbm, kr_hbm, vr_hbm, kp_hbm, vp_hbm, o_hbm, g_hbm, len_ref,
    dq_out, dkr_out, dvr_out, dkp_out, dvp_out,
    kv, q3, g3, o3, qt, gt, kt, pd, part, sums, got, ext, m8, l8,
    ag_send, ag_recv, rs_send, rs_recv, in_sem, kv_sem,
):
    c2 = scale * LOG2E
    rows = q3.shape[1]
    head_dim = q3.shape[2]
    chunk = 2 * head_dim
    me = lax.axis_index("seq")

    def at(step):
        return {"seq": lax.rem(me + step + n, n)}

    barrier = pltpu.get_barrier_semaphore()
    for step in (1, -1, 2, -2):
        pl.semaphore_signal(barrier, inc=1, device_id=at(step), device_id_type=MESH)

    own = 8 * chunk
    local = [
        pltpu.make_async_copy(kp_hbm, kv.at[0, pl.ds(own, 128)], kv_sem.at[0]),
        pltpu.make_async_copy(vp_hbm, kv.at[1, pl.ds(own, 128)], kv_sem.at[1]),
        pltpu.make_async_copy(kr_hbm, kv.at[0, pl.ds(0, chunk)], kv_sem.at[2]),
        pltpu.make_async_copy(vr_hbm, kv.at[1, pl.ds(0, chunk)], kv_sem.at[3]),
    ]
    for copy in local:
        copy.start()
    loads = []
    for h in range(heads):
        for a, (src, dst) in enumerate(((q_hbm, q3), (g_hbm, g3), (o_hbm, o3))):
            copy = pltpu.make_async_copy(
                src.at[:, pl.ds(h * head_dim, head_dim)], dst.at[h], in_sem.at[a, h]
            )
            copy.start()
            loads.append(copy)

    def slot(d, way):
        if d == 8:
            return pl.ds(own + 128 + 64 * way, 64)
        return pl.ds(d * chunk + 128 * way, 128)

    def gather(kind, d, way):
        pa = PARENT[d]
        step = (d - pa) * (1 if way == 0 else -1)
        if pa == 0:
            src = (kp_hbm, vp_hbm)[kind]
        elif d == 8:
            src = kv.at[kind, pl.ds(pa * chunk + 128 * way + 64 * way, 64)]
        else:
            src = kv.at[kind, slot(pa, way)]
        return pltpu.make_async_remote_copy(
            src_ref=src, dst_ref=kv.at[kind, slot(d, way)],
            send_sem=ag_send.at[kind, way, d - 1], recv_sem=ag_recv.at[kind, way, d - 1],
            device_id=at(step), device_id_type=MESH,
        )

    def arrive(kind, d):
        for way in range(2):
            gather(kind, d, way).wait_recv()

    pl.semaphore_wait(barrier, 4)

    def run_round(i):
        for item in ROUNDS[i]:
            here, _, there = item.partition(">")
            if here:
                arrive("kv".index(here[0]), int(here[1]))
            for name in there.split(","):
                for way in range(2):
                    if name:
                        gather("kv".index(name[0]), int(name[1]), way).start()

    run_round(0)

    lane = lax.broadcasted_iota(jnp.int32, (chunk, 128), 1)
    ext[...] = jnp.where(lane < 3, -1.0, 0.0).astype(BF16)
    qt[pl.ds(head_dim, 128), :] = jnp.zeros((128, qt.shape[1]), BF16)
    gt[pl.ds(head_dim, 128), :] = jnp.zeros((128, gt.shape[1]), BF16)
    m8[...] = jnp.full(m8.shape, LOW, F32)
    l8[...] = jnp.zeros(l8.shape, F32)
    length = len_ref[0]
    live = lax.broadcasted_iota(jnp.int32, (rows, head_dim), 0) < length

    def cols(h):
        if isinstance(h, int):
            return pl.ds(h * rows, rows)
        return pl.ds(pl.multiple_of(h * rows, rows), rows)

    def prepare(h):
        g = jnp.where(live, g3[h].astype(F32), 0.0)
        o = o3[h].astype(F32)
        g3[h] = g.astype(BF16)
        g_t = g.T
        delta = jnp.sum(g_t * o.T, axis=0, keepdims=True)
        gt[pl.ds(0, head_dim), cols(h)] = g_t.astype(BF16)
        gt[pl.ds(head_dim, 16), cols(h)] = split3(delta)

    for h in range(heads):
        loads[3 * h].wait()
        qt[pl.ds(0, head_dim), cols(h)] = q3[h].astype(F32).T.astype(BF16)

    def causal():
        key = lax.broadcasted_iota(jnp.int32, (chunk, rows), 0)
        token = lax.broadcasted_iota(jnp.int32, (chunk, rows), 1)
        return key <= token

    def chunk_rows(c):
        if isinstance(c, int):
            return pl.ds(c * chunk, chunk)
        return pl.ds(pl.multiple_of(c * chunk, chunk), chunk)

    def first_pass(c, w=1, masked=False):
        keys = kv[0, pl.ds(c * chunk, w * chunk)]
        for h in range(heads):
            s = dot(keys, qt[pl.ds(0, head_dim), cols(h)])
            if masked:
                s = jnp.where(causal(), s, LOW)
            s = s.reshape(w * chunk // 8, 8, rows)
            old = m8[h]
            new = jnp.maximum(old, jnp.max(s, axis=0))
            e = jnp.exp2((s - new[None]) * c2)
            l8[h] = l8[h] * jnp.exp2((old - new) * c2) + jnp.sum(e, axis=0)
            m8[h] = new

    def turn(c):
        kt[:, chunk_rows(c)] = kv[0, chunk_rows(c)].astype(F32).T.astype(BF16)

    def finish_first():
        def step(h, carry):
            m = jnp.max(m8[h], axis=0, keepdims=True)
            total = jnp.sum(l8[h] * jnp.exp2((m8[h] - m) * c2), axis=0, keepdims=True)
            lse = m + jnp.log(total) * (1.0 / scale)
            qt[pl.ds(head_dim, 16), cols(h)] = split3(lse)
            return carry

        lax.fori_loop(0, heads, step, 0, unroll=HU)

    def probs(c, w=1, masked=False):
        r = pl.ds(c * chunk, chunk * w)
        keys = jnp.concatenate([kv[0, r], jnp.concatenate([ext[...]] * w, axis=0)], axis=1)
        for h in range(heads):
            p = jnp.exp2(dot(keys, qt[:, cols(h)]) * c2)
            if masked:
                p = jnp.where(causal(), p, 0.0)
            pd[r, cols(h)] = p.astype(BF16)
        part[1, r] = dot(pd[r, :], g3[...].reshape(heads * rows, head_dim))

    def dscores(c, w=1):
        r = pl.ds(c * chunk, chunk * w)
        values = jnp.concatenate([kv[1, r], jnp.concatenate([ext[...]] * w, axis=0)], axis=1)
        for h in range(heads):
            dp = dot(values, gt[:, cols(h)])
            pd[r, cols(h)] = (pd[r, cols(h)].astype(F32) * dp).astype(BF16)
        part[0, r] = dot(pd[r, :], q3[...].reshape(heads * rows, head_dim))

    local[2].wait()
    local[3].wait()
    local[0].wait()
    local[1].wait()

    def pair(hi, body):
        def step(i, carry):
            body(hi - i)
            return carry

        lax.fori_loop(0, 2, step, 0)

    for i in (1, 2, 3, 4):
        run_round(i)
        if i == 1:
            first_pass(0, masked=True)
        if i == 2:
            for copy in loads[1::3] + loads[2::3]:
                copy.wait()
            for h in range(heads):
                prepare(h)
        first_pass(2 * i - 1, 2)
        if i < 4:
            pair(2 * i, turn)
    finish_first()

    factor = (scale, 1.0)

    def mine(kind, d, way):
        if d == 0:
            r = pl.ds(own, 128)
        elif d == 8:
            r = pl.ds(own + 128 + 64 * way, 64)
        else:
            r = pl.ds(d * chunk + 128 * (1 - way), 128)
        return part[kind, r] * factor[kind]

    def rs_rows(d, way):
        return pl.ds(64 * way, 64) if d == 8 else pl.ds(0, 128)

    def scatter(kind, d, way):
        step = (d - PARENT[d]) * (1 if way == 0 else -1)
        r = rs_rows(d, way)
        return pltpu.make_async_remote_copy(
            src_ref=sums.at[kind, way, d - 1, r], dst_ref=got.at[kind, way, d - 1, r],
            send_sem=rs_send.at[kind, way, d - 1], recv_sem=rs_recv.at[kind, way, d - 1],
            device_id=at(step), device_id_type=MESH,
        )

    def total(kind, d, way, acc):
        for child in (8, 7, 6, 5, 4, 3, 2, 1):
            if PARENT[child] != d:
                continue
            scatter(kind, child, way).wait_recv()
            term = got[kind, way, child - 1, rs_rows(child, way)].astype(F32)
            if child == 8:
                if way == 0:
                    acc = jnp.concatenate([acc[:64] + term, acc[64:]], axis=0)
                else:
                    acc = jnp.concatenate([acc[:64], acc[64:] + term], axis=0)
            else:
                acc = acc + term
        return acc

    def send_sum(kind, d):
        for way in range(2):
            acc = total(kind, d, way, mine(kind, d, way))
            sums[kind, way, d - 1, rs_rows(d, way)] = acc.astype(BF16)
            scatter(kind, d, way).start()

    def last_values():
        for d in (1, 3, 5, 8, 7):
            arrive(1, d)

    steps = (
        lambda: probs(7, 2),
        lambda: (last_values(), dscores(7, 2)),
        lambda: probs(5, 2),
        lambda: dscores(5, 2),
        lambda: probs(3, 2),
        lambda: dscores(3, 2),
        lambda: probs(1, 2),
        lambda: dscores(1, 2),
        lambda: probs(0, masked=True),
        lambda: (pair(8, turn), turn(0), dscores(0)),
    )
    for i, step in enumerate(steps):
        step()
        for name in PLAN[i]:
            send_sum("kv".index(name[0]), int(name[1]))

    dkr_out[...] = (part[0, pl.ds(0, chunk)] * scale).astype(BF16)
    dvr_out[...] = part[1, pl.ds(0, chunk)].astype(BF16)
    for h in range(heads):
        d_q = dot(kt[...], pd[:, cols(h)]) * scale
        dq_out[:, pl.ds(h * head_dim, head_dim)] = d_q.T.astype(BF16)

    for kind in (1, 0):
        acc = mine(kind, 0, 0)
        for way in range(2):
            acc = total(kind, 0, way, acc)
        (dkp_out, dvp_out)[kind][...] = acc.astype(BF16)

    for kind in range(2):
        for d in range(1, 9):
            for way in range(2):
                gather(kind, d, way).wait_send()
                scatter(kind, d, way).wait_send()


def deliver(*refs):
    copies = [pltpu.make_async_copy(refs[i], refs[5 + i], refs[10].at[i]) for i in range(5)]
    for copy in copies:
        copy.start()
    for copy in copies:
        copy.wait()


def per_device(n, queries, resp_keys, resp_values, prompt_keys, prompt_values, outputs, out_grads, lengths):
    rows = queries.shape[0]
    head_dim = resp_keys.shape[1]
    heads = queries.shape[1] // head_dim
    scale = head_dim ** (-0.5)
    keys = n * prompt_keys.shape[0] + rows
    wide = heads * rows
    any_spec = pl.BlockSpec(memory_space=pl.ANY)
    vmem_spec = pl.BlockSpec(memory_space=pltpu.VMEM)
    outs = (queries, resp_keys, resp_values, prompt_keys, prompt_values)
    inputs = tuple(
        pltpu.with_memory_space_constraint(x, pltpu.HBM) for x in outs + (outputs, out_grads)
    )
    results = pl.pallas_call(
        functools.partial(kernel, n, heads, scale),
        out_shape=tuple(pltpu.VMEM(x.shape, BF16) for x in outs),
        in_specs=[any_spec] * 7 + [pl.BlockSpec(memory_space=pltpu.SMEM)],
        out_specs=(vmem_spec,) * 5,
        scratch_shapes=[
            pltpu.VMEM((2, keys, head_dim), BF16),
            pltpu.VMEM((heads, rows, head_dim), BF16),
            pltpu.VMEM((heads, rows, head_dim), BF16),
            pltpu.VMEM((heads, rows, head_dim), BF16),
            pltpu.VMEM((2 * head_dim, wide), BF16),
            pltpu.VMEM((2 * head_dim, wide), BF16),
            pltpu.VMEM((head_dim, keys), BF16),
            pltpu.VMEM((keys, wide), BF16),
            pltpu.VMEM((2, keys, head_dim), F32),
            pltpu.VMEM((2, 2, 8, 128, head_dim), BF16),
            pltpu.VMEM((2, 2, 8, 128, head_dim), BF16),
            pltpu.VMEM((2 * head_dim, 128), BF16),
            pltpu.VMEM((heads, 8, rows), F32),
            pltpu.VMEM((heads, 8, rows), F32),
            pltpu.SemaphoreType.DMA((2, 2, 8)),
            pltpu.SemaphoreType.DMA((2, 2, 8)),
            pltpu.SemaphoreType.DMA((2, 2, 8)),
            pltpu.SemaphoreType.DMA((2, 2, 8)),
            pltpu.SemaphoreType.DMA((3, heads)),
            pltpu.SemaphoreType.DMA((4,)),
        ],
        compiler_params=pltpu.CompilerParams(
            collective_id=0, has_side_effects=True, vmem_limit_bytes=44 * 1024 * 1024
        ),
    )(*inputs, lengths)
    return pl.pallas_call(
        deliver,
        out_shape=tuple(pltpu.HBM(x.shape, BF16) for x in outs),
        in_specs=[vmem_spec] * 5,
        out_specs=(any_spec,) * 5,
        scratch_shapes=[pltpu.SemaphoreType.DMA((5,))],
    )(*(pltpu.with_memory_space_constraint(x, pltpu.VMEM) for x in results))


def solution(mesh):
    spec = P(("grp", "seq"), "kv")
    return jax.shard_map(
        functools.partial(per_device, mesh.shape["seq"]),
        mesh=mesh,
        in_specs=(spec,) * 7 + (P(("grp", "seq")),),
        out_specs=(spec,) * 5,
        check_vma=False,
    )
```

time: 74.2 us -> 54.5 us (0.73); the launches traced: 72.7 us -> 54.2 us
  local copies, waits for them, and re-layouts: 9.59 us -> 0 us
  Pallas kernels: 61.8 us -> 52.8 us
    unnamed x19 -> x0, local copies, waits for them, and re-layouts: 9.59 us -> none
    pallas_call x1 -> x2, Pallas kernels: 61.8 us -> 52.8 us  [the longest x1 51.9 us: per_device(): pl.pallas_call(functools.partial(kernel, n, heads, scale), out_shape=tupl...]
where the time goes in v2:
time: 54.5 us; the launch traced here: 54.2 us
  Pallas kernels  52.8 us (97%)
  between operations  1.47 us (3%)
    pallas_call x1, Pallas kernels, per_device(): pl.pallas_call(functools.partial(kernel, n, heads, scale), out_shape=tupl...  51.9 us

profile of v2, /device:TPU:6, one launch (start us, length us, event | category | flops | bytes accessed | tf_op | source)
XLA Modules:
  0.0 54.2 jit_solution(5853275840429951386)
XLA Ops:
  1.3 51.9 %shard_map.119 = (bf16[256,1024]{1,0:T(8,128)(2,1)S(1)}, bf16[256,128]{1,0:T(8,128)(2,1)S(1)}, bf16[256,128]{1,0:T(8,128)(2,1)S(1)}, bf16[128,128]{1,0:T(8,128)(2,1)S(1)}, bf16[128,128]{1,0:T(8,128)(2,1)S(1)}) custom-call(bf16[256,1024]{1,0:T(8,128)(2,1)} %q_hbm.1, bf16[256,128]{1,0:T(8,128)(2,1)} %kr_hbm.1, bf16[256,128]{1,0:T(8,128)(2,1)} %vr_hbm.1, ...), custom_call_target="tpu_custom_call" | custom-call | tf_op jit(solution)/shard_map/pallas_call | solution.py:339
  53.2 0.9 %shard_map.120 = (bf16[256,1024]{1,0:T(8,128)(2,1)}, bf16[256,128]{1,0:T(8,128)(2,1)}, bf16[256,128]{1,0:T(8,128)(2,1)}, bf16[128,128]{1,0:T(8,128)(2,1)}, bf16[128,128]{1,0:T(8,128)(2,1)}) custom-call(bf16[256,1024]{1,0:T(8,128)(2,1)S(1)} %get-tuple-element.10.refs_0_, bf16[256,128]{1,0:T(8,128)(2,1)S(1)} %get-tuple-element.11.refs_1_, ...), custom_call_target="tpu_custom_call" | custom-call | tf_op jit(solution)/shard_map/pallas_call | solution.py:370

commit v3 on v2

--- a/solution.py
+++ b/solution.py
@@ -68,7 +68,50 @@
     for step in (1, -1, 2, -2):
         pl.semaphore_signal(barrier, inc=1, device_id=at(step), device_id_type=MESH)
 
-    own = 8 * chunk
+    own = chunk
+    near = own + 128
+
+    def first(d):
+        return near + (d - 1) * chunk
+
+    def slot(d, way):
+        if d == 8:
+            return pl.ds(first(d) + 64 * way, 64)
+        return pl.ds(first(d) + 128 * way, 128)
+
+    def gather(kind, d, way):
+        pa = PARENT[d]
+        step = (d - pa) * (1 if way == 0 else -1)
+        if pa == 0:
+            src = (kp_hbm, vp_hbm)[kind]
+        elif d == 8:
+            src = kv.at[kind, pl.ds(first(pa) + 128 * way + 64 * way, 64)]
+        else:
+            src = kv.at[kind, slot(pa, way)]
+        return pltpu.make_async_remote_copy(
+            src_ref=src, dst_ref=kv.at[kind, slot(d, way)],
+            send_sem=ag_send.at[kind, way, d - 1], recv_sem=ag_recv.at[kind, way, d - 1],
+            device_id=at(step), device_id_type=MESH,
+        )
+
+    def arrive(kind, d):
+        for way in range(2):
+            gather(kind, d, way).wait_recv()
+
+    pl.semaphore_wait(barrier, 4)
+
+    def run_round(i):
+        for item in ROUNDS[i]:
+            here, _, there = item.partition(">")
+            if here:
+                arrive("kv".index(here[0]), int(here[1]))
+            for name in there.split(","):
+                for way in range(2):
+                    if name:
+                        gather("kv".index(name[0]), int(name[1]), way).start()
+
+    run_round(0)
+
     local = [
         pltpu.make_async_copy(kp_hbm, kv.at[0, pl.ds(own, 128)], kv_sem.at[0]),
         pltpu.make_async_copy(vp_hbm, kv.at[1, pl.ds(own, 128)], kv_sem.at[1]),
@@ -86,45 +129,7 @@
             copy.start()
             loads.append(copy)
 
-    def slot(d, way):
-        if d == 8:
-            return pl.ds(own + 128 + 64 * way, 64)
-        return pl.ds(d * chunk + 128 * way, 128)
-
-    def gather(kind, d, way):
-        pa = PARENT[d]
-        step = (d - pa) * (1 if way == 0 else -1)
-        if pa == 0:
-            src = (kp_hbm, vp_hbm)[kind]
-        elif d == 8:
-            src = kv.at[kind, pl.ds(pa * chunk + 128 * way + 64 * way, 64)]
-        else:
-            src = kv.at[kind, slot(pa, way)]
-        return pltpu.make_async_remote_copy(
-            src_ref=src, dst_ref=kv.at[kind, slot(d, way)],
-            send_sem=ag_send.at[kind, way, d - 1], recv_sem=ag_recv.at[kind, way, d - 1],
-            device_id=at(step), device_id_type=MESH,
-        )
-
-    def arrive(kind, d):
-        for way in range(2):
-            gather(kind, d, way).wait_recv()
-
-    pl.semaphore_wait(barrier, 4)
-
-    def run_round(i):
-        for item in ROUNDS[i]:
-            here, _, there = item.partition(">")
-            if here:
-                arrive("kv".index(here[0]), int(here[1]))
-            for name in there.split(","):
-                for way in range(2):
-                    if name:
-                        gather("kv".index(name[0]), int(name[1]), way).start()
-
-    run_round(0)
-
-    lane = lax.broadcasted_iota(jnp.int32, (chunk, 128), 1)
+    lane = lax.broadcasted_iota(jnp.int32, ext.shape, 1)
     ext[...] = jnp.where(lane < 3, -1.0, 0.0).astype(BF16)
     qt[pl.ds(head_dim, 128), :] = jnp.zeros((128, qt.shape[1]), BF16)
     gt[pl.ds(head_dim, 128), :] = jnp.zeros((128, gt.shape[1]), BF16)
@@ -151,31 +156,27 @@
         loads[3 * h].wait()
         qt[pl.ds(0, head_dim), cols(h)] = q3[h].astype(F32).T.astype(BF16)
 
-    def causal():
-        key = lax.broadcasted_iota(jnp.int32, (chunk, rows), 0)
-        token = lax.broadcasted_iota(jnp.int32, (chunk, rows), 1)
-        return key <= token
-
-    def chunk_rows(c):
-        if isinstance(c, int):
-            return pl.ds(c * chunk, chunk)
-        return pl.ds(pl.multiple_of(c * chunk, chunk), chunk)
-
-    def first_pass(c, w=1, masked=False):
-        keys = kv[0, pl.ds(c * chunk, w * chunk)]
+    def allowed():
+        key = lax.broadcasted_iota(jnp.int32, (near, rows), 0)
+        token = lax.broadcasted_iota(jnp.int32, (near, rows), 1)
+        return jnp.logical_or(key <= token, key >= chunk)
+
+    def first_pass(start, size, masked=False):
+        keys = kv[0, pl.ds(start, size)]
         for h in range(heads):
             s = dot(keys, qt[pl.ds(0, head_dim), cols(h)])
             if masked:
-                s = jnp.where(causal(), s, LOW)
-            s = s.reshape(w * chunk // 8, 8, rows)
+                s = jnp.where(allowed(), s, LOW)
+            s = s.reshape(size // 8, 8, rows)
             old = m8[h]
             new = jnp.maximum(old, jnp.max(s, axis=0))
             e = jnp.exp2((s - new[None]) * c2)
             l8[h] = l8[h] * jnp.exp2((old - new) * c2) + jnp.sum(e, axis=0)
             m8[h] = new
 
-    def turn(c):
-        kt[:, chunk_rows(c)] = kv[0, chunk_rows(c)].astype(F32).T.astype(BF16)
+    def turn(start, size):
+        r = pl.ds(start, size)
+        kt[:, r] = kv[0, r].astype(F32).T.astype(BF16)
 
     def finish_first():
         def step(h, carry):
@@ -187,48 +188,41 @@
 
         lax.fori_loop(0, heads, step, 0, unroll=HU)
 
-    def probs(c, w=1, masked=False):
-        r = pl.ds(c * chunk, chunk * w)
-        keys = jnp.concatenate([kv[0, r], jnp.concatenate([ext[...]] * w, axis=0)], axis=1)
+    def probs(start, size, masked=False):
+        r = pl.ds(start, size)
+        keys = jnp.concatenate([kv[0, r], ext[pl.ds(0, size)]], axis=1)
         for h in range(heads):
             p = jnp.exp2(dot(keys, qt[:, cols(h)]) * c2)
             if masked:
-                p = jnp.where(causal(), p, 0.0)
+                p = jnp.where(allowed(), p, 0.0)
             pd[r, cols(h)] = p.astype(BF16)
         part[1, r] = dot(pd[r, :], g3[...].reshape(heads * rows, head_dim))
 
-    def dscores(c, w=1):
-        r = pl.ds(c * chunk, chunk * w)
-        values = jnp.concatenate([kv[1, r], jnp.concatenate([ext[...]] * w, axis=0)], axis=1)
+    def dscores(start, size):
+        r = pl.ds(start, size)
+        values = jnp.concatenate([kv[1, r], ext[pl.ds(0, size)]], axis=1)
         for h in range(heads):
             dp = dot(values, gt[:, cols(h)])
             pd[r, cols(h)] = (pd[r, cols(h)].astype(F32) * dp).astype(BF16)
         part[0, r] = dot(pd[r, :], q3[...].reshape(heads * rows, head_dim))
 
-    local[2].wait()
-    local[3].wait()
-    local[0].wait()
-    local[1].wait()
-
-    def pair(hi, body):
-        def step(i, carry):
-            body(hi - i)
-            return carry
-
-        lax.fori_loop(0, 2, step, 0)
-
+    for copy in local:
+        copy.wait()
+
+    pairs = ((first(1), 2 * chunk), (first(3), 2 * chunk), (first(5), 2 * chunk), (first(7), chunk + 128))
     for i in (1, 2, 3, 4):
         run_round(i)
         if i == 1:
-            first_pass(0, masked=True)
+            first_pass(0, near, masked=True)
+            turn(0, near)
         if i == 2:
             for copy in loads[1::3] + loads[2::3]:
                 copy.wait()
             for h in range(heads):
                 prepare(h)
-        first_pass(2 * i - 1, 2)
+        first_pass(*pairs[i - 1])
         if i < 4:
-            pair(2 * i, turn)
+            turn(*pairs[i - 1])
     finish_first()
 
     factor = (scale, 1.0)
@@ -237,9 +231,9 @@
         if d == 0:
             r = pl.ds(own, 128)
         elif d == 8:
-            r = pl.ds(own + 128 + 64 * way, 64)
+            r = pl.ds(first(d) + 64 * way, 64)
         else:
-            r = pl.ds(d * chunk + 128 * (1 - way), 128)
+            r = pl.ds(first(d) + 128 * (1 - way), 128)
         return part[kind, r] * factor[kind]
 
     def rs_rows(d, way):
@@ -280,16 +274,16 @@
             arrive(1, d)
 
     steps = (
-        lambda: probs(7, 2),
-        lambda: (last_values(), dscores(7, 2)),
-        lambda: probs(5, 2),
-        lambda: dscores(5, 2),
-        lambda: probs(3, 2),
-        lambda: dscores(3, 2),
-        lambda: probs(1, 2),
-        lambda: dscores(1, 2),
-        lambda: probs(0, masked=True),
-        lambda: (pair(8, turn), turn(0), dscores(0)),
+        lambda: probs(*pairs[3]),
+        lambda: (last_values(), dscores(*pairs[3])),
+        lambda: probs(*pairs[2]),
+        lambda: dscores(*pairs[2]),
+        lambda: probs(*pairs[1]),
+        lambda: dscores(*pairs[1]),
+        lambda: probs(*pairs[0]),
+        lambda: dscores(*pairs[0]),
+        lambda: probs(0, near, masked=True),
+        lambda: (dscores(0, near), turn(*pairs[3])),
     )
     for i, step in enumerate(steps):
         step()
@@ -353,7 +347,7 @@
             pltpu.VMEM((2, keys, head_dim), F32),
             pltpu.VMEM((2, 2, 8, 128, head_dim), BF16),
             pltpu.VMEM((2, 2, 8, 128, head_dim), BF16),
-            pltpu.VMEM((2 * head_dim, 128), BF16),
+            pltpu.VMEM((4 * head_dim, 128), BF16),
             pltpu.VMEM((heads, 8, rows), F32),
             pltpu.VMEM((heads, 8, rows), F32),
             pltpu.SemaphoreType.DMA((2, 2, 8)),

time: 54.5 us -> 54 us (level)
  Pallas kernels: 52.8 us -> 52.2 us
    pallas_call x1, Pallas kernels: 51.9 us -> 51.3 us  [per_device(): pl.pallas_call(functools.partial(kernel, n, heads, scale), out_shape=tupl...]
where the time goes in v3:
time: 54 us; the launch traced here: 53.6 us
  Pallas kernels  52.2 us (97%)
  between operations  1.45 us (3%)
    pallas_call x1, Pallas kernels, per_device(): pl.pallas_call(functools.partial(kernel, n, heads, scale), out_shape=tupl...  51.3 us

profile of v3, /device:TPU:6, one launch (start us, length us, event | category | flops | bytes accessed | tf_op | source)
XLA Modules:
  0.0 53.6 jit_solution(9291421519726465503)
XLA Ops:
  1.3 51.3 %shard_map.119 = (bf16[256,1024]{1,0:T(8,128)(2,1)S(1)}, bf16[256,128]{1,0:T(8,128)(2,1)S(1)}, bf16[256,128]{1,0:T(8,128)(2,1)S(1)}, bf16[128,128]{1,0:T(8,128)(2,1)S(1)}, bf16[128,128]{1,0:T(8,128)(2,1)S(1)}) custom-call(bf16[256,1024]{1,0:T(8,128)(2,1)} %q_hbm.1, bf16[256,128]{1,0:T(8,128)(2,1)} %kr_hbm.1, bf16[256,128]{1,0:T(8,128)(2,1)} %vr_hbm.1, ...), custom_call_target="tpu_custom_call" | custom-call | tf_op jit(solution)/shard_map/pallas_call | solution.py:333
  52.6 0.9 %shard_map.120 = (bf16[256,1024]{1,0:T(8,128)(2,1)}, bf16[256,128]{1,0:T(8,128)(2,1)}, bf16[256,128]{1,0:T(8,128)(2,1)}, bf16[128,128]{1,0:T(8,128)(2,1)}, bf16[128,128]{1,0:T(8,128)(2,1)}) custom-call(bf16[256,1024]{1,0:T(8,128)(2,1)S(1)} %get-tuple-element.10.refs_0_, bf16[256,128]{1,0:T(8,128)(2,1)S(1)} %get-tuple-element.11.refs_1_, ...), custom_call_target="tpu_custom_call" | custom-call | tf_op jit(solution)/shard_map/pallas_call | solution.py:364

commit v4 on v3

--- a/solution.py
+++ b/solution.py
@@ -161,7 +161,12 @@
         token = lax.broadcasted_iota(jnp.int32, (near, rows), 1)
         return jnp.logical_or(key <= token, key >= chunk)
 
-    def first_pass(start, size, masked=False):
+    def finish(h, peaks, sums_of):
+        m = jnp.max(peaks, axis=0, keepdims=True)
+        all_of = jnp.sum(sums_of * jnp.exp2((peaks - m) * c2), axis=0, keepdims=True)
+        qt[pl.ds(head_dim, 16), cols(h)] = split3(m + jnp.log(all_of) * (1.0 / scale))
+
+    def first_pass(start, size, masked=False, last=False):
         keys = kv[0, pl.ds(start, size)]
         for h in range(heads):
             s = dot(keys, qt[pl.ds(0, head_dim), cols(h)])
@@ -171,22 +176,16 @@
             old = m8[h]
             new = jnp.maximum(old, jnp.max(s, axis=0))
             e = jnp.exp2((s - new[None]) * c2)
-            l8[h] = l8[h] * jnp.exp2((old - new) * c2) + jnp.sum(e, axis=0)
-            m8[h] = new
+            sums_of = l8[h] * jnp.exp2((old - new) * c2) + jnp.sum(e, axis=0)
+            if last:
+                finish(h, new, sums_of)
+            else:
+                l8[h] = sums_of
+                m8[h] = new
 
     def turn(start, size):
         r = pl.ds(start, size)
         kt[:, r] = kv[0, r].astype(F32).T.astype(BF16)
-
-    def finish_first():
-        def step(h, carry):
-            m = jnp.max(m8[h], axis=0, keepdims=True)
-            total = jnp.sum(l8[h] * jnp.exp2((m8[h] - m) * c2), axis=0, keepdims=True)
-            lse = m + jnp.log(total) * (1.0 / scale)
-            qt[pl.ds(head_dim, 16), cols(h)] = split3(lse)
-            return carry
-
-        lax.fori_loop(0, heads, step, 0, unroll=HU)
 
     def probs(start, size, masked=False):
         r = pl.ds(start, size)
@@ -220,10 +219,9 @@
                 copy.wait()
             for h in range(heads):
                 prepare(h)
-        first_pass(*pairs[i - 1])
+        first_pass(*pairs[i - 1], last=i == 4)
         if i < 4:
             turn(*pairs[i - 1])
-    finish_first()
 
     factor = (scale, 1.0)
 
@@ -310,7 +308,12 @@
 
 
 def deliver(*refs):
-    copies = [pltpu.make_async_copy(refs[i], refs[5 + i], refs[10].at[i]) for i in range(5)]
+    copies = [pltpu.make_async_copy(refs[i], refs[5 + i], refs[10].at[i]) for i in range(1, 5)]
+    part = refs[0].shape[0] // 4
+    for i in range(4):
+        r = pl.ds(i * part, part)
+        sem = refs[10].at[0 if i == 0 else 4 + i]
+        copies.insert(0, pltpu.make_async_copy(refs[0].at[r], refs[5].at[r], sem))
     for copy in copies:
         copy.start()
     for copy in copies:
@@ -366,7 +369,7 @@
         out_shape=tuple(pltpu.HBM(x.shape, BF16) for x in outs),
         in_specs=[vmem_spec] * 5,
         out_specs=(any_spec,) * 5,
-        scratch_shapes=[pltpu.SemaphoreType.DMA((5,))],
+        scratch_shapes=[pltpu.SemaphoreType.DMA((8,))],
     )(*(pltpu.with_memory_space_constraint(x, pltpu.VMEM) for x in results))
 
 

time: 54 us -> 54 us (level)
  no operation moved by 1% of the time
where the time goes in v4:
time: 54 us; the launch traced here: 53.7 us
  Pallas kernels  52.2 us (97%)
  between operations  1.45 us (3%)
    pallas_call x1, Pallas kernels, per_device(): pl.pallas_call(functools.partial(kernel, n, heads, scale), out_shape=tupl...  51.3 us

profile of v4, /device:TPU:6, one launch (start us, length us, event | category | flops | bytes accessed | tf_op | source)
XLA Modules:
  0.0 53.7 jit_solution(10764131637311598835)
XLA Ops:
  1.3 51.3 %shard_map.119 = (bf16[256,1024]{1,0:T(8,128)(2,1)S(1)}, bf16[256,128]{1,0:T(8,128)(2,1)S(1)}, bf16[256,128]{1,0:T(8,128)(2,1)S(1)}, bf16[128,128]{1,0:T(8,128)(2,1)S(1)}, bf16[128,128]{1,0:T(8,128)(2,1)S(1)}) custom-call(bf16[256,1024]{1,0:T(8,128)(2,1)} %q_hbm.1, bf16[256,128]{1,0:T(8,128)(2,1)} %kr_hbm.1, bf16[256,128]{1,0:T(8,128)(2,1)} %vr_hbm.1, ...), custom_call_target="tpu_custom_call" | custom-call | tf_op jit(solution)/shard_map/pallas_call | solution.py:336
  52.6 0.9 %shard_map.120 = (bf16[256,1024]{1,0:T(8,128)(2,1)}, bf16[256,128]{1,0:T(8,128)(2,1)}, bf16[256,128]{1,0:T(8,128)(2,1)}, bf16[128,128]{1,0:T(8,128)(2,1)}, bf16[128,128]{1,0:T(8,128)(2,1)}) custom-call(bf16[256,1024]{1,0:T(8,128)(2,1)S(1)} %get-tuple-element.10.refs_0_, bf16[256,128]{1,0:T(8,128)(2,1)S(1)} %get-tuple-element.11.refs_1_, ...), custom_call_target="tpu_custom_call" | custom-call | tf_op jit(solution)/shard_map/pallas_call | solution.py:367
